TPU v7x, 32 devices: a whole 2x2x4 slice. The times are simulated.
32 devices in a mesh: grp: 4 (over z), loc: 2 (over x), tp: 4 (over y, core).
Axes of the slice: x: 2, y: 2, z: 4, core: 2. Of those that a mesh axis runs over, the one named last changes fastest.
Arguments:
- resid_in: bfloat16 [256, 4096], P(('grp', 'loc'), 'tp'), may hold values from -140 to 140
- attn_heads: bfloat16 [256, 16384], P('grp', 'loc'), may hold values from -6 to 6
- out_proj: bfloat16 [16384, 4096], P('loc', 'tp'), may hold values from -0.046875 to 0.046875
- norm_gain: float32 [4096], P('tp'), may hold values from 0.25 to 1.75
- expert_ids: int32 [256, 8], P(('grp', 'loc')), may hold values from 0 to 7, as said below
- gate_scores: int32 [256, 8], P(('grp', 'loc')), may hold values from 1 to 1023
- w_gate: bfloat16 [8, 4096, 1024], P(('grp', 'loc'), 'tp'), may hold values from -0.09375 to 0.09375
- w_up: bfloat16 [8, 4096, 1024], P(('grp', 'loc'), 'tp'), may hold values from -0.09375 to 0.09375
- w_down: bfloat16 [8, 1024, 4096], P(('grp', 'loc'), None, 'tp'), may hold values from -0.1875 to 0.1875
Outputs:
- layer_out: bfloat16 [256, 4096], P(('grp', 'loc'), 'tp')
Inputs may be any that keep to these rules, and one draw needn't show every extreme that they name: `expert_ids`: each row names 8 different experts: 2 in each of 4 different groups, expert e being in group e // 2. In each aligned block of 32 rows (the tokens of one grp and loc position) no group is named by more than 32 rows and no expert by more than 32 rows; in every block some group and some expert reach these bounds, and some expert reaches 32 in every block.
All inputs are finite; a program needn't handle non-finite values.
Results may differ from a plain program's by a relative error of at most 0.0095.
Values may be sent and summed in bfloat16 or wider, within the bound.
A program may use at most 64 MiB of HBM per device.

v0:
```python
import jax
import jax.numpy as jnp
from jax import lax
from jax.sharding import PartitionSpec as P

D = 4096
KEEP = 4
PER = 2


route_scale = 2.5
norm_eps = 1e-06


def local(resid_in, attn_heads, out_proj, norm_gain, expert_ids, gate_scores, w_gate, w_up, w_down):
    group_count = lax.axis_size("grp")
    local_count = lax.axis_size("loc")
    block_rows = resid_in.shape[0]
    lane_width = resid_in.shape[1]
    expert_total = group_count * local_count
    spread = group_count // KEEP
    group_cap = min(block_rows, 2 * block_rows // spread)
    expert_cap = PER * group_cap // local_count
    slot_count = expert_total * expert_cap
    attn_out = lax.psum_scatter(
        jnp.dot(attn_heads, out_proj, preferred_element_type=jnp.float32).astype(jnp.bfloat16),
        "loc",
        scatter_dimension=0,
        tiled=True,
    ).astype(jnp.float32)
    mixed = resid_in.astype(jnp.float32) + attn_out
    square_sum = lax.psum(jnp.sum(mixed * mixed, axis=1), "tp")
    inverse_rms = lax.rsqrt(square_sum / D + norm_eps)
    normed = (mixed * inverse_rms[:, None] * norm_gain).astype(jnp.bfloat16)
    scores = gate_scores.astype(jnp.float32)
    route_weight = route_scale * scores / jnp.sum(scores, axis=1, keepdims=True)
    expert_hit = (expert_ids[:, :, None] == jnp.arange(expert_total, dtype=jnp.int32)).astype(
        jnp.float32
    )
    named_expert = jnp.sum(expert_hit, axis=1)
    expert_weight = jnp.sum(expert_hit * route_weight[:, :, None], axis=1)
    earlier = (jnp.arange(block_rows)[:, None] > jnp.arange(block_rows)[None, :]).astype(
        jnp.float32
    )
    before = jnp.dot(earlier, named_expert, precision=lax.Precision.HIGHEST)
    position = jnp.sum(expert_hit * before[:, None, :], axis=2).astype(jnp.int32)
    slot_index = expert_ids * expert_cap + position
    slot_hit = (slot_index[:, :, None] == jnp.arange(slot_count, dtype=jnp.int32)).astype(
        jnp.float32
    )
    group_ids = expert_ids // local_count
    group_hit = (group_ids[:, :, None] == jnp.arange(group_count, dtype=jnp.int32)).astype(
        jnp.float32
    )
    group_named = jnp.minimum(jnp.sum(group_hit, axis=1), 1.0)
    group_before = jnp.dot(earlier, group_named, precision=lax.Precision.HIGHEST)
    group_place = group_named[:, :, None] * (
        group_before[:, :, None] == jnp.arange(group_cap, dtype=jnp.float32)
    ).astype(jnp.float32)
    expert_rank = jnp.where(named_expert > 0, before, -1.0).reshape(
        block_rows, group_count, local_count
    )
    slot_info = (
        jnp.einsum("rgc,rgl->gcl", group_place, expert_rank + 1.0, precision=lax.Precision.HIGHEST)
        - 1.0
    )
    placement = jnp.sum(slot_hit, axis=1).astype(jnp.bfloat16)
    outgoing = jnp.einsum("rs,rd->sd", placement, normed, preferred_element_type=jnp.float32)
    outgoing = outgoing.astype(jnp.bfloat16).reshape(
        group_count, local_count, expert_cap, lane_width
    )
    arrived = lax.all_to_all(
        lax.all_to_all(outgoing, "grp", split_axis=0, concat_axis=0, tiled=True),
        "loc",
        split_axis=1,
        concat_axis=1,
        tiled=True,
    )
    slot_rows = arrived.reshape(slot_count, lane_width)
    gate_part = jnp.dot(slot_rows, w_gate[0], preferred_element_type=jnp.float32)
    up_part = jnp.dot(slot_rows, w_up[0], preferred_element_type=jnp.float32)
    gate_pre, up_pre = (
        lax.psum(gate_part.astype(jnp.bfloat16), "tp").astype(jnp.float32),
        lax.psum(up_part.astype(jnp.bfloat16), "tp").astype(jnp.float32),
    )
    active = (jax.nn.silu(gate_pre) * up_pre).astype(jnp.bfloat16)
    expert_out = jnp.dot(active, w_down[0], preferred_element_type=jnp.float32).astype(jnp.bfloat16)
    out_blocks = expert_out.reshape(group_count, local_count, expert_cap, lane_width)
    slot_weight = jnp.einsum(
        "rgc,rgl->gcl",
        group_place,
        expert_weight.reshape(block_rows, group_count, local_count),
        precision=lax.Precision.HIGHEST,
    )
    rank_there, weight_there = (
        lax.all_to_all(slot_info, "grp", split_axis=0, concat_axis=0, tiled=True),
        lax.all_to_all(slot_weight, "grp", split_axis=0, concat_axis=0, tiled=True),
    )
    at_group = lax.all_to_all(out_blocks, "loc", split_axis=1, concat_axis=1, tiled=True)
    picks = (rank_there[:, :, :, None] == jnp.arange(expert_cap, dtype=jnp.float32)).astype(
        jnp.float32
    )
    picks = picks * weight_there[:, :, :, None]
    summed = jnp.einsum(
        "gclp,glpd->gcd", picks, at_group.astype(jnp.float32), precision=lax.Precision.HIGHEST
    ).astype(jnp.bfloat16)
    at_owner = lax.all_to_all(summed, "grp", split_axis=0, concat_axis=0, tiled=True)
    layer_out = mixed + jnp.einsum(
        "rgc,gcd->rd", group_place, at_owner.astype(jnp.float32), precision=lax.Precision.HIGHEST
    )
    return layer_out.astype(jnp.bfloat16)


def solution(mesh):
    placed = (
        P(("grp", "loc"), "tp"),
        P("grp", "loc"),
        P("loc", "tp"),
        P("tp"),
        P(("grp", "loc"), None),
        P(("grp", "loc"), None),
        P(("grp", "loc"), "tp", None),
        P(("grp", "loc"), "tp", None),
        P(("grp", "loc"), None, "tp"),
    )
    return jax.shard_map(
        local, mesh=mesh, in_specs=placed, out_specs=P(("grp", "loc"), "tp"), check_vma=False
    )
```

profile of v0, /device:TPU:0, one launch (start us, length us, event | category | flops | bytes accessed | tf_op | source)
XLA Modules:
  0.0 139.7 jit_solution(8360859615918029383)
XLA Ops:
  6.5 0.0 reduce-scatter.2.cloned.1.call-start
  6.6 9.9 %convolution_convert_fusion.1 = bf16[64,1024]{1,0:T(8,128)(2,1)} fusion(bf16[64,8192]{1,0:T(8,128)(2,1)} %param.10, bf16[8192,1024]{1,0:T(8,128)(2,1)} %param.11), kind=kOutput, calls=%fused_computation.14 | convolution fusion | flops 1073807360 | bytes 17956864 | tf_op jit(solution)/shard_map/dot_general | solution.py:26
  16.5 0.0 reduce-scatter.2.cloned.1.call-update
  16.6 0.1 select_add_fusion
  16.8 0.1 copy.46
  16.8 0.2 convert_reduce_fusion
  17.0 12.6 %reduce-scatter.2.cloned.1.call-done = bf16[32,1024]{1,0:T(8,128)(2,1)} async-done(((bf16[64,1024]{1,0:T(8,128)(2,1)}), bf16[32,1024]{1,0:T(8,128)(2,1)}) %reduce-scatter.2.cloned.1.call-update) | async-done | bytes 65552 | tf_op jit(solution)/shard_map/reduce_scatter | solution.py:25
  29.6 1.0 multiply_reduce_fusion
  30.6 6.5 %psum.21 = f32[32]{0:T(128)S(1)} all-reduce(f32[32]{0:T(128)S(1)} %multiply_reduce_fusion), channel_id=1, replica_groups=mesh['grp'=4,'loc'=2,'tp'=4] {'tp'}, use_global_device_ids=true, to_apply=%region_8.9 | all-reduce | flops 32 | bytes 256 | tf_op jit(solution)/shard_map/psum | solution.py:32
  37.1 1.2 convolution_convert_fusion
  38.3 18.1 %all_to_all.30 = bf16[4,2,32,1024]{3,2,1,0:T(8,128)(2,1)S(1)} all-to-all(bf16[4,2,32,1024]{3,2,1,0:T(8,128)(2,1)S(1)} %bitcast.40), channel_id=1, replica_groups=mesh['grp'=4,'loc'=2,'tp'=4] {'grp'}, dimensions={0} | all-to-all | bytes 1048576 | tf_op jit(solution)/shard_map/all_to_all | solution.py:73
  56.4 0.8 copy.47
  57.2 3.5 %all-to-all-start.3 = ((bf16[4,2,32,1024]{3,2,0,1:T(8,128)(2,1)}), bf16[4,2,32,1024]{3,2,0,1:T(8,128)(2,1)S(1)}, u32[]{:S(2)}, u32[]{:S(2)}) async-start(bf16[4,2,32,1024]{3,2,0,1:T(8,128)(2,1)} %copy.47), calls=%async_computation.4 | async-start | bytes 1048576 | tf_op jit(solution)/shard_map/all_to_all | solution.py:72
  60.7 0.0 all-reduce.3.cloned.1.call-start
  60.8 0.1 fusion.47
  60.9 6.8 %all-to-all-done.3 = bf16[4,2,32,1024]{3,2,0,1:T(8,128)(2,1)S(1)} async-done(((bf16[4,2,32,1024]{3,2,0,1:T(8,128)(2,1)}), bf16[4,2,32,1024]{3,2,0,1:T(8,128)(2,1)S(1)}, u32[]{:S(2)}, u32[]{:S(2)}) %all-to-all-start.3) | async-done | bytes 524320 | tf_op jit(solution)/shard_map/all_to_all | solution.py:72
  67.8 1.5 %fusion.9 = bf16[256,1024]{1,0:T(8,128)(2,1)} fusion(bf16[256,1024]{1,0:T(8,128)(2,1)S(1)} %bitcast.41, bf16[1,1024,1024]{2,1,0:T(8,128)(2,1)S(1)} %copy-done), kind=kOutput, calls=%fused_computation.9 | convolution fusion | flops 537133056 | bytes 3145728 | tf_op jit(solution)/shard_map/dot_general | solution.py:81
  69.3 0.0 copy-done.6
  69.3 1.5 %fusion.6 = bf16[256,1024]{1,0:T(8,128)(2,1)} fusion(bf16[256,1024]{1,0:T(8,128)(2,1)S(1)} %bitcast.42, bf16[1,1024,1024]{2,1,0:T(8,128)(2,1)S(1)} %copy-done.6), kind=kOutput, calls=%fused_computation.8 | convolution fusion | flops 537133056 | bytes 3145728 | tf_op jit(solution)/shard_map/dot_general | solution.py:80
  70.9 0.0 all-reduce.3.cloned.1.call-update
  70.9 0.9 convolution_add_fusion
  71.8 3.4 %all-to-all-start = ((f32[4,32,2]{1,2,0:T(2,128)}), f32[4,32,2]{1,2,0:T(2,128)S(1)}, u32[]{:S(2)}, u32[]{:S(2)}) async-start(f32[4,32,2]{1,2,0:T(2,128)} %convolution_add_fusion), calls=%async_computation.1 | async-start | bytes 8192 | tf_op jit(solution)/shard_map/all_to_all | solution.py:96
  75.1 0.9 fusion.28
  76.0 4.7 %all-to-all-done = f32[4,32,2]{1,2,0:T(2,128)S(1)} async-done(((f32[4,32,2]{1,2,0:T(2,128)}), f32[4,32,2]{1,2,0:T(2,128)S(1)}, u32[]{:S(2)}, u32[]{:S(2)}) %all-to-all-start) | async-done | bytes 1056 | tf_op jit(solution)/shard_map/all_to_all | solution.py:96
  80.7 3.2 %all-to-all-start.1 = ((f32[4,32,2]{1,2,0:T(2,128)}), f32[4,32,2]{1,2,0:T(2,128)S(1)}, u32[]{:S(2)}, u32[]{:S(2)}) async-start(f32[4,32,2]{1,2,0:T(2,128)} %fusion.28), calls=%async_computation.2 | async-start | bytes 8192 | tf_op jit(solution)/shard_map/all_to_all | solution.py:97
  84.0 22.1 %all-reduce.3.cloned.1.call-done = (bf16[256,1024]{1,0:T(8,128)(2,1)}, bf16[256,1024]{1,0:T(8,128)(2,1)}) async-done(((bf16[256,1024]{1,0:T(8,128)(2,1)}, bf16[256,1024]{1,0:T(8,128)(2,1)}), (bf16[256,1024]{1,0:T(8,128)(2,1)}, bf16[256,1024]{1,0:T(8,128)(2,1)})) %all-reduce.3.cloned.1.call-update) | async-done | bytes 1048592 | tf_op jit(solution)/shard_map/psum | solution.py:84
  106.0 2.7 %fusion.12 = bf16[256,1024]{1,0:T(8,128)(2,1)S(1)} fusion(bf16[1,1024,1024]{2,1,0:T(8,128)(2,1)} %param.17, bf16[256,1024]{1,0:T(8,128)(2,1)} %get-tuple-element.7, bf16[256,1024]{1,0:T(8,128)(2,1)} %get-tuple-element.8), kind=kOutput, calls=%fused_computation.10 | convolution fusion | flops 539230208 | bytes 3670016 | tf_op jit(solution)/shard_map/dot_general | solution.py:87
  108.8 0.0 all-to-all-done.1
  108.8 10.5 %all_to_all.31 = bf16[4,2,32,1024]{3,2,0,1:T(8,128)(2,1)S(1)} all-to-all(bf16[4,2,32,1024]{3,2,0,1:T(8,128)(2,1)S(1)} %copy.49), channel_id=1, replica_groups=mesh['grp'=4,'loc'=2,'tp'=4] {'loc'}, dimensions={1} | all-to-all | bytes 1048576 | tf_op jit(solution)/shard_map/all_to_all | solution.py:99
  119.3 0.5 fusion.15
  119.9 11.9 %all_to_all.32 = bf16[4,32,1024]{2,1,0:T(8,128)(2,1)S(1)} all-to-all(bf16[4,32,1024]{2,1,0:T(8,128)(2,1)S(1)} %fusion.15), channel_id=1, replica_groups=mesh['grp'=4,'loc'=2,'tp'=4] {'grp'}, dimensions={0} | all-to-all | bytes 524288 | tf_op jit(solution)/shard_map/all_to_all | solution.py:107
  131.8 1.0 fusion.17
  (23 shorter events, 0.2 us)
Async XLA Ops:
  6.5 61.3 %copy-start = (bf16[1,1024,1024]{2,1,0:T(8,128)(2,1)S(1)}, bf16[1,1024,1024]{2,1,0:T(8,128)(2,1)}, u32[]{:S(2)}) copy-start(bf16[1,1024,1024]{2,1,0:T(8,128)(2,1)} %param.16) | copy-start | bytes 6291460
  6.5 10.0 %copy-start.4 = (s32[32,8]{0,1:T(8,128)S(1)}, s32[32,8]{0,1:T(8,128)}, u32[]{:S(2)}) copy-start(s32[32,8]{0,1:T(8,128)} %param.14) | copy-start | bytes 3076
  6.5 10.0 %copy-start.3 = (s32[32,8]{0,1:T(8,128)S(1)}, s32[32,8]{0,1:T(8,128)}, u32[]{:S(2)}) copy-start(s32[32,8]{0,1:T(8,128)} %param.13) | copy-start | bytes 3076
  6.5 23.1 %copy-start.1 = (bf16[32,1024]{1,0:T(8,128)(2,1)S(1)}, bf16[32,1024]{1,0:T(8,128)(2,1)}, u32[]{:S(2)}) copy-start(bf16[32,1024]{1,0:T(8,128)(2,1)} %param.9) | copy-start | bytes 196612
  6.5 30.6 %copy-start.5 = (f32[1024]{0:T(1024)S(1)}, f32[1024]{0:T(1024)}, u32[]{:S(2)}) copy-start(f32[1024]{0:T(1024)} %param.12) | copy-start | bytes 12292
  6.5 23.0 %reduce-scatter.2.cloned.1.call-start = ((), (), s32[]{:S(2)}) async-start(), calls=%async_computation.7 | async-start | bytes 196608 | tf_op jit(solution)/shard_map/reduce_scatter | solution.py:25
  57.2 10.5 %all-to-all-start.3 = ((bf16[4,2,32,1024]{3,2,0,1:T(8,128)(2,1)}), bf16[4,2,32,1024]{3,2,0,1:T(8,128)(2,1)S(1)}, u32[]{:S(2)}, u32[]{:S(2)}) async-start(bf16[4,2,32,1024]{3,2,0,1:T(8,128)(2,1)} %copy.47), calls=%async_computation.4 | async-start | bytes 1048576 | tf_op jit(solution)/shard_map/all_to_all | solution.py:72
  60.7 45.3 %all-reduce.3.cloned.1.call-start = ((), (), s32[]{:S(2)}) async-start(), calls=%async_computation.8 | async-start | bytes 2097152 | tf_op jit(solution)/shard_map/psum | solution.py:84
  67.7 1.6 %copy-start.6 = (bf16[1,1024,1024]{2,1,0:T(8,128)(2,1)S(1)}, bf16[1,1024,1024]{2,1,0:T(8,128)(2,1)}, u32[]{:S(2)}) copy-start(bf16[1,1024,1024]{2,1,0:T(8,128)(2,1)} %param.15) | copy-start | bytes 6291460
  71.8 8.9 %all-to-all-start = ((f32[4,32,2]{1,2,0:T(2,128)}), f32[4,32,2]{1,2,0:T(2,128)S(1)}, u32[]{:S(2)}, u32[]{:S(2)}) async-start(f32[4,32,2]{1,2,0:T(2,128)} %convolution_add_fusion), calls=%async_computation.1 | async-start | bytes 8192 | tf_op jit(solution)/shard_map/all_to_all | solution.py:96
  80.7 28.1 %all-to-all-start.1 = ((f32[4,32,2]{1,2,0:T(2,128)}), f32[4,32,2]{1,2,0:T(2,128)S(1)}, u32[]{:S(2)}, u32[]{:S(2)}) async-start(f32[4,32,2]{1,2,0:T(2,128)} %fusion.28), calls=%async_computation.2 | async-start | bytes 8192 | tf_op jit(solution)/shard_map/all_to_all | solution.py:97
  108.8 23.0 %copy-start.2 = (bf16[32,1024]{1,0:T(8,128)(2,1)S(1)}, bf16[32,1024]{1,0:T(8,128)(2,1)}, u32[]{:S(2)}) copy-start(bf16[32,1024]{1,0:T(8,128)(2,1)} %reduce-scatter.2.cloned.1.call-done) | copy-start | bytes 196612
Sparse Core Ops, SparseCore 0:
  16.6 12.9 reduce-scatter.1
  71.0 34.9 all-reduce.2
where the time goes:
time: 140 us
  blocking collectives  47 us (34%)
  waiting for transfers between devices  46.3 us (33%)
  matrix products  20.4 us (15%)
  between operations  13.6 us (10%)
  starting transfers between devices  10.2 us (7%)
    psum x1, waiting for transfers between devices, local(): lax.psum(up_part.astype(jnp.bfloat16), 'tp').astype(jnp.float32)  22.1 us
    all_to_all x1, blocking collectives, local(): lax.all_to_all(outgoing, 'grp', split_axis=0, concat_axis=0, tiled=True)  18.1 us
    reduce_scatter x1, waiting for transfers between devices, local(): lax.psum_scatter(jnp.dot(attn_heads, out_proj, preferred_element_type=jnp...  12.6 us
    all_to_all x1, blocking collectives, local(): lax.all_to_all(summed, 'grp', split_axis=0, concat_axis=0, tiled=True)  11.9 us
    all_to_all x1, blocking collectives, local(): lax.all_to_all(out_blocks, 'loc', split_axis=1, concat_axis=1, tiled=True)  10.5 us
    dot_general x1, matrix products, local(): jnp.dot(attn_heads, out_proj, preferred_element_type=jnp.float32)  9.89 us
    all_to_all x1, waiting for transfers between devices, local(): lax.all_to_all(lax.all_to_all(outgoing, 'grp', split_axis=0, concat_axis=...  6.83 us
    psum x1, blocking collectives, local(): square_sum = lax.psum(jnp.sum(mixed * mixed, axis=1), 'tp')  6.52 us
  transfers between devices with their start and end apart: 5, of which 4 were waited for; matrix products, arithmetic and copies ran while one was open for 4% of the time, Pallas kernels for 0%

commit v1 on v0

--- a/solution.py
+++ b/solution.py
@@ -1,7 +1,14 @@
+import functools
+
 import jax
 import jax.numpy as jnp
 from jax import lax
+from jax.experimental import pallas as pl
+from jax.experimental.pallas import tpu as pltpu
 from jax.sharding import PartitionSpec as P
+
+MESH = pl.DeviceIdType.MESH
+LANES = 128
 
 D = 4096
 KEEP = 4
@@ -12,7 +19,7 @@
 norm_eps = 1e-06
 
 
-def local(resid_in, attn_heads, out_proj, norm_gain, expert_ids, gate_scores, w_gate, w_up, w_down):
+def routed(resid_in, attn_heads, out_proj, norm_gain, expert_ids, gate_scores, w_gate, w_up, w_down):
     group_count = lax.axis_size("grp")
     local_count = lax.axis_size("loc")
     block_rows = resid_in.shape[0]
@@ -111,6 +118,330 @@
     return layer_out.astype(jnp.bfloat16)
 
 
+def dense_kernel(
+    sizes, resid, heads, proj, gain, ids, scores, w_gate, w_up, w_down, out,
+    heads_v, proj_v, gate_v, up_v, down_v, rs_out, rs_in, mixed, rows, sq_out, sq_in, info,
+    core_out, core_in, own, y_out, y_in, active, pair_out, pair_in, part_out, part_in,
+    local_sem, send_sem, recv_sem,
+):
+    groups, tp_count, parts, out_parts = sizes
+    block, width = resid.shape
+    depth = heads.shape[1]
+    ff = gate_v.shape[1]
+    piece = width // parts
+    out_piece = width // out_parts
+    fpiece = ff // tp_count
+    tall = groups * block
+    g, l, t = lax.axis_index("grp"), lax.axis_index("loc"), lax.axis_index("tp")
+    core, y = lax.rem(t, 2), t // 2
+    core_peer = t + 1 - 2 * core
+    y_peer = t + 2 - 4 * y
+    diagonal = core_peer + 2 - 4 * y
+    at_core, at_y, at_x = {"tp": core_peer}, {"tp": y_peer}, {"loc": 1 - l}
+
+    def at_group(step):
+        return {"grp": lax.rem(g + step + groups, groups)}
+
+    barrier = pltpu.get_barrier_semaphore()
+    friends = [{"tp": lax.rem(t + r, tp_count)} for r in range(1, tp_count)]
+    friends += [at_group(d) for d in range(1, groups)]
+    friends += [{**at_group(d), **at_x} for d in range(groups)]
+    for friend in friends:
+        pl.semaphore_signal(barrier, inc=1, device_id=friend, device_id_type=MESH)
+
+    local_count = [0]
+
+    def fetch(src, dst):
+        copy = pltpu.make_async_copy(src, dst, local_sem.at[local_count[0]])
+        local_count[0] += 1
+        return copy
+
+    started = []
+    remote_count = [0]
+
+    def send(src, dst, device):
+        n = remote_count[0]
+        remote_count[0] += 1
+        copy = pltpu.make_async_remote_copy(
+            src_ref=src, dst_ref=dst, send_sem=send_sem.at[n], recv_sem=recv_sem.at[n],
+            device_id=device, device_id_type=MESH,
+        )
+        copy.start()
+        started.append(copy)
+        return copy
+
+    get_heads = fetch(heads, heads_v)
+    half = depth // 2
+    get_proj = [
+        [
+            fetch(
+                proj.at[pl.ds(k * half, half), pl.ds(c * piece, piece)],
+                proj_v.at[c, pl.ds(k * half, half)],
+            )
+            for k in range(2)
+        ]
+        for c in range(parts)
+    ]
+    get_gate = fetch(w_gate.at[0], gate_v)
+    get_up = fetch(w_up.at[0], up_v)
+    get_down = fetch(w_down.at[0], down_v)
+    get_heads.start()
+    for c in range(min(2, parts)):
+        for copy in get_proj[c]:
+            copy.start()
+
+    lane = lax.broadcasted_iota(jnp.int32, (block, LANES), 1)
+    score = scores[...].astype(jnp.float32)
+    score = route_scale * score / jnp.sum(score, axis=1, keepdims=True)
+    weights = jnp.zeros((block, LANES), jnp.float32)
+    for k in range(ids.shape[1]):
+        weights += jnp.where(ids[:, k : k + 1] == lane, score[:, k : k + 1], 0.0)
+
+    rs, spread, forward = {}, {}, {}
+    keep = [None] * parts
+    square = [jnp.zeros((block, 1), jnp.float32)]
+
+    def settle(c):
+        columns = pl.ds(c * piece, piece)
+        rs[c].wait_recv()
+        total = resid[:, columns].astype(jnp.float32) + (keep[c] + rs_in[c].astype(jnp.float32))
+        mixed[:, columns] = total
+        square[0] += jnp.sum(total * total, axis=1, keepdims=True)
+        rows[0, 0, :, columns] = (total * gain[:, columns]).astype(jnp.bfloat16)
+        mine = rows.at[0, 0, :, columns]
+        forward[c, 0] = send(mine, rows.at[1, 0, :, columns], at_x)
+        for d in range(groups - 1, 0, -1):
+            spread[c, d] = send(mine, rows.at[0, d, :, columns], at_group(d))
+
+    def pass_on(c):
+        columns = pl.ds(c * piece, piece)
+        for d in range(1, groups):
+            spread[c, d].wait_recv()
+            here = rows.at[0, d, :, columns]
+            forward[c, d] = send(here, rows.at[1, d, :, columns], at_x)
+
+    for c in range(parts):
+        if c == 0:
+            get_heads.wait()
+        for copy in get_proj[c]:
+            copy.wait()
+        if c + 2 < parts:
+            for copy in get_proj[c + 2]:
+                copy.start()
+        if c + 2 == parts or parts == 1:
+            get_gate.start()
+            get_up.start()
+            get_down.start()
+        share = jnp.dot(heads_v[...], proj_v[c], preferred_element_type=jnp.float32)
+        low, high = share[:block], share[block:]
+        keep[c] = jnp.where(l == 0, low, high)
+        rs_out[c] = jnp.where(l == 0, high, low).astype(jnp.bfloat16)
+        if c == 0:
+            pl.semaphore_wait(barrier, len(friends))
+        rs[c] = send(rs_out.at[c], rs_in.at[c], at_x)
+        if c >= 1:
+            settle(c - 1)
+        if c >= 2:
+            pass_on(c - 2)
+    settle(parts - 1)
+
+    sq_out[...] = jnp.broadcast_to(square[0], sq_out.shape)
+    sums = [
+        send(sq_out, sq_in.at[r - 1], {"tp": lax.rem(t + r, tp_count)})
+        for r in range(1, tp_count)
+    ]
+    if parts >= 2:
+        pass_on(parts - 2)
+    pass_on(parts - 1)
+    total_square = sq_out[...]
+    for r, copy in enumerate(sums):
+        copy.wait_recv()
+        total_square += sq_in[r]
+    inverse = lax.rsqrt(total_square / (width * tp_count) + norm_eps)
+    expert_count = ids.shape[1]
+    info[0, 0] = jnp.where(lane < expert_count, weights, inverse)
+    told = {}
+    for d in range(groups):
+        told[1, d] = send(info.at[0, 0], info.at[1, d], {**at_group(d), **at_x})
+    for d in range(1, groups):
+        told[0, d] = send(info.at[0, 0], info.at[0, d], at_group(d))
+
+    get_gate.wait()
+    get_up.wait()
+
+    def pair(side, q):
+        x = rows[side].reshape(tall, width)
+        columns = pl.ds(pl.multiple_of(q * fpiece, fpiece), fpiece)
+        return (
+            jnp.dot(x, gate_v[:, columns], preferred_element_type=jnp.float32),
+            jnp.dot(x, up_v[:, columns], preferred_element_type=jnp.float32),
+        )
+
+    over_core, over_y, from_y, from_core, relay = {}, {}, {}, {}, {}
+
+    def give(side):
+        if side == 1:
+            for c in range(parts):
+                for d in range(groups):
+                    forward[c, d].wait_recv()
+        for n, q in enumerate((diagonal, core_peer)):
+            for m, value in enumerate(pair(side, q)):
+                core_out[side, n, m] = value.astype(jnp.bfloat16)
+            over_core[side, n] = send(core_out.at[side, n], core_in.at[side, n], at_core)
+
+    def hold(side):
+        for n, q in enumerate((y_peer, t)):
+            for m, value in enumerate(pair(side, q)):
+                own[side, n, m] = value
+
+    def cross(side):
+        over_core[side, 0].wait_recv()
+        y_out[side] = (own[side, 0] + core_in[side, 0].astype(jnp.float32)).astype(jnp.bfloat16)
+        over_y[side] = send(y_out.at[side], y_in.at[side], at_y)
+
+    def activate(side):
+        over_core[side, 1].wait_recv()
+        kept = own[side, 1] + core_in[side, 1].astype(jnp.float32)
+        for d in range(groups):
+            if (side, d) in told:
+                told[side, d].wait_recv()
+        known = info[side].reshape(tall, LANES)
+        known_lane = lax.broadcasted_iota(jnp.int32, (tall, LANES), 1)
+        expert = g * 2 + l
+        scale = known[:, expert_count : expert_count + 1]
+        weight = jnp.sum(jnp.where(known_lane == expert, known, 0.0), axis=1, keepdims=True)
+        over_y[side].wait_recv()
+        pre = (kept + y_in[side].astype(jnp.float32)) * scale
+        gate_pre, up_pre = pre[0], pre[1]
+        value = gate_pre / (1.0 + jnp.exp(-gate_pre)) * up_pre * weight
+        active[side, 0] = value.astype(jnp.bfloat16)
+        from_y[side] = send(active.at[side, 0], active.at[side, 2], at_y)
+        from_core[side] = send(active.at[side, 0], active.at[side, 1], at_core)
+
+    def hand_over(side):
+        from_y[side].wait_recv()
+        relay[side] = send(active.at[side, 2], active.at[side, 3], at_core)
+
+    def down(side, c):
+        columns = pl.ds(c * out_piece, out_piece)
+        total = None
+        for n, q in enumerate((t, core_peer, y_peer, diagonal)):
+            if c == 0 and n == 1:
+                from_core[side].wait_recv()
+            if c == 0 and n == 3:
+                relay[side].wait_recv()
+            part = jnp.dot(
+                active[side, n],
+                down_v[pl.ds(pl.multiple_of(q * fpiece, fpiece), fpiece), columns],
+                preferred_element_type=jnp.float32,
+            )
+            total = part if total is None else total + part
+        return total
+
+    give(1)
+    hold(1)
+    give(0)
+    cross(1)
+    hold(0)
+    cross(0)
+    get_down.wait()
+    activate(1)
+    activate(0)
+    hand_over(1)
+    across, home = {}, {}
+    for c in range(out_parts):
+        pair_out[c] = down(1, c).astype(jnp.bfloat16)
+        across[c] = send(pair_out.at[c], pair_in.at[c], at_x)
+        if c == 0:
+            hand_over(0)
+    for c in range(out_parts):
+        summed = down(0, c)
+        across[c].wait_recv()
+        summed += pair_in[c].astype(jnp.float32)
+        part_out[c] = summed.astype(jnp.bfloat16).reshape(groups, block, out_piece)
+        for d in range(1, groups):
+            home[c, d] = send(part_out.at[c, d], part_in.at[c, d - 1], at_group(-d))
+    for c in range(out_parts):
+        columns = pl.ds(c * out_piece, out_piece)
+        total = mixed[:, columns] + part_out[c, 0].astype(jnp.float32)
+        for d in range(1, groups):
+            home[c, d].wait_recv()
+            total += part_in[c, d - 1].astype(jnp.float32)
+        out[:, columns] = total.astype(out.dtype)
+    for copy in started:
+        copy.wait_send()
+
+
+def dense(resid_in, attn_heads, out_proj, norm_gain, expert_ids, gate_scores, w_gate, w_up, w_down):
+    groups, tp_count = lax.axis_size("grp"), lax.axis_size("tp")
+    block, width = resid_in.shape
+    heads_shape = attn_heads.shape
+    ff = w_gate.shape[2]
+    fpiece = ff // tp_count
+    tall = groups * block
+    parts, out_parts = 4, 2
+    piece, out_piece = width // parts, width // out_parts
+    bf16, f32 = jnp.bfloat16, jnp.float32
+    local_copies = 4 + 2 * parts
+    remote_copies = (
+        parts + parts * (2 * groups - 1) + (tp_count - 1) + (2 * groups - 1) + 4 + 2 + 6
+        + out_parts * groups
+    )
+    vmem = pl.BlockSpec(memory_space=pltpu.VMEM)
+    anywhere = pl.BlockSpec(memory_space=pl.ANY)
+    return pl.pallas_call(
+        functools.partial(dense_kernel, (groups, tp_count, parts, out_parts)),
+        out_shape=jax.ShapeDtypeStruct(resid_in.shape, bf16),
+        in_specs=[vmem, anywhere, anywhere, vmem, vmem, vmem, anywhere, anywhere, anywhere],
+        out_specs=vmem,
+        scratch_shapes=[
+            pltpu.VMEM(heads_shape, bf16),
+            pltpu.VMEM((parts, heads_shape[1], piece), bf16),
+            pltpu.VMEM((width, ff), bf16),
+            pltpu.VMEM((width, ff), bf16),
+            pltpu.VMEM((ff, width), bf16),
+            pltpu.VMEM((parts, block, piece), bf16),
+            pltpu.VMEM((parts, block, piece), bf16),
+            pltpu.VMEM((block, width), f32),
+            pltpu.VMEM((2, groups, block, width), bf16),
+            pltpu.VMEM((block, LANES), f32),
+            pltpu.VMEM((tp_count - 1, block, LANES), f32),
+            pltpu.VMEM((2, groups, block, LANES), f32),
+            pltpu.VMEM((2, 2, 2, tall, fpiece), bf16),
+            pltpu.VMEM((2, 2, 2, tall, fpiece), bf16),
+            pltpu.VMEM((2, 2, 2, tall, fpiece), f32),
+            pltpu.VMEM((2, 2, tall, fpiece), bf16),
+            pltpu.VMEM((2, 2, tall, fpiece), bf16),
+            pltpu.VMEM((2, 4, tall, fpiece), bf16),
+            pltpu.VMEM((out_parts, tall, out_piece), bf16),
+            pltpu.VMEM((out_parts, tall, out_piece), bf16),
+            pltpu.VMEM((out_parts, groups, block, out_piece), bf16),
+            pltpu.VMEM((out_parts, groups - 1, block, out_piece), bf16),
+            pltpu.SemaphoreType.DMA((local_copies,)),
+            pltpu.SemaphoreType.DMA((remote_copies,)),
+            pltpu.SemaphoreType.DMA((remote_copies,)),
+        ],
+        compiler_params=pltpu.CompilerParams(
+            collective_id=0, has_side_effects=True, vmem_limit_bytes=52 * 1024 * 1024
+        ),
+    )(
+        resid_in, attn_heads, out_proj, norm_gain.reshape(1, width), expert_ids, gate_scores,
+        w_gate, w_up, w_down,
+    )
+
+
+def local(*arrays):
+    expert_ids = arrays[4]
+    expert_total = lax.axis_size("grp") * lax.axis_size("loc")
+    if (
+        expert_ids.shape[1] == expert_total
+        and lax.axis_size("loc") == 2
+        and lax.axis_size("tp") == 4
+    ):
+        return dense(*arrays)
+    return routed(*arrays)
+
+
 def solution(mesh):
     placed = (
         P(("grp", "loc"), "tp"),

time: 140 us -> 56.7 us (0.41)
  Pallas kernels: 0 us -> 51.5 us
  blocking collectives: 47 us -> 0 us
  waiting for transfers between devices: 46.3 us -> 0 us
  matrix products: 20.4 us -> 0 us
  between operations: 13.6 us -> 0.01 us
  starting transfers between devices: 10.2 us -> 0 us
  local copies, waits for them, and re-layouts: 1.03 us -> 4.9 us
    pallas_call x0 -> x1, Pallas kernels: none -> 51.5 us  [dense(): pl.pallas_call(functools.partial(dense_kernel, (groups, tp_count, parts,...]
    all_to_all x3 -> x0, blocking collectives: 40.5 us -> none  [the longest x1 18.1 us: local(): lax.all_to_all(outgoing, 'grp', split_axis=0, concat_axis=0, tiled=True)]
    psum x1 -> x0, waiting for transfers between devices: 22.1 us -> none  [local(): lax.psum(up_part.astype(jnp.bfloat16), 'tp').astype(jnp.float32)]
    dot_general x11 -> x0, matrix products: 20.4 us -> none  [the longest x1 9.89 us: local(): jnp.dot(attn_heads, out_proj, preferred_element_type=jnp.float32)]
    reduce_scatter x1 -> x0, waiting for transfers between devices: 12.6 us -> none  [local(): lax.psum_scatter(jnp.dot(attn_heads, out_proj, preferred_element_type=jnp...]
    all_to_all x3 -> x0, waiting for transfers between devices: 11.6 us -> none  [the longest x1 6.83 us: local(): lax.all_to_all(lax.all_to_all(outgoing, 'grp', split_axis=0, concat_axis=...]
    all_to_all x3 -> x0, starting transfers between devices: 10.1 us -> none  [the longest x1 3.49 us: local(): lax.all_to_all(lax.all_to_all(outgoing, 'grp', split_axis=0, concat_axis=...]
    psum x1 -> x0, blocking collectives: 6.52 us -> none  [local(): square_sum = lax.psum(jnp.sum(mixed * mixed, axis=1), 'tp')]
  transfers between devices with their start and end apart: 5 -> 0, of which waited for: 4 -> 0; matrix products, arithmetic and copies ran while one was open for 4% -> 0% of each run, Pallas kernels for 0% -> 0%
where the time goes in v1:
time: 56.7 us; the launch traced here: 56.4 us
  Pallas kernels  51.5 us (91%)
  local copies, waits for them, and re-layouts  4.9 us (9%)
    pallas_call x1, Pallas kernels, dense(): pl.pallas_call(functools.partial(dense_kernel, (groups, tp_count, parts,...  51.5 us
    unnamed x9, local copies, waits for them, and re-layouts  4.9 us

profile of v1, /device:TPU:0, one launch (start us, length us, event | category | flops | bytes accessed | tf_op | source)
XLA Modules:
  0.0 56.4 jit_solution(1874294473246224152)
XLA Ops:
  0.0 0.8 %copy.10.ids = s32[32,8]{1,0:T(8,128)S(1)} copy(s32[32,8]{0,1:T(8,128)} %param.13) | data formatting | bytes 2048 | tf_op args[4]
  0.8 0.8 %copy.11.scores = s32[32,8]{1,0:T(8,128)S(1)} copy(s32[32,8]{0,1:T(8,128)} %param.14) | data formatting | bytes 2048 | tf_op args[5]
  1.5 0.0 copy-start
  1.5 1.2 %copy-done = bf16[64,8192]{1,0:T(8,128)(2,1)S(1)} copy-done((bf16[64,8192]{1,0:T(8,128)(2,1)S(1)}, bf16[64,8192]{1,0:T(8,128)(2,1)}, u32[]{:S(2)}) %copy-start) | copy-done | bytes 1048600
  2.7 0.0 copy-start.1
  2.8 0.8 %copy-done.1 = bf16[32,1024]{1,0:T(8,128)(2,1)S(1)} copy-done((bf16[32,1024]{1,0:T(8,128)(2,1)S(1)}, bf16[32,1024]{1,0:T(8,128)(2,1)}, u32[]{:S(2)}) %copy-start.1) | copy-done | bytes 65560
  3.6 0.0 copy-start.2
  3.6 0.7 %copy-done.2 = f32[1024]{0:T(1024)S(1)} copy-done((f32[1024]{0:T(1024)S(1)}, f32[1024]{0:T(1024)}, u32[]{:S(2)}) %copy-start.2) | copy-done | bytes 4120
  4.3 51.5 %shard_map.91 = bf16[32,1024]{1,0:T(8,128)(2,1)S(1)} custom-call(bf16[32,1024]{1,0:T(8,128)(2,1)S(1)} %copy-done.1, bf16[64,8192]{1,0:T(8,128)(2,1)S(1)} %copy-done, bf16[8192,1024]{1,0:T(8,128)(2,1)} %proj.1, f32[1,1024]{1,0:T(1,128)S(1)} %bitcast.1, s32[32,8]{1,0:T(8,128)S(1)} %copy.10.ids, s32[32,8]{1,0:T(8,128)S(1)} %copy.11.scores, ...), custom_call_target="tpu_custom_call" | custom-call | tf_op jit(solution)/shard_map/pallas_call | solution.py:392
  55.8 0.6 %copy.13 = bf16[32,1024]{1,0:T(8,128)(2,1)} copy(bf16[32,1024]{1,0:T(8,128)(2,1)S(1)} %shard_map.91) | data formatting | bytes 131072
Async XLA Ops:
  1.5 1.2 %copy-start = (bf16[64,8192]{1,0:T(8,128)(2,1)S(1)}, bf16[64,8192]{1,0:T(8,128)(2,1)}, u32[]{:S(2)}) copy-start(bf16[64,8192]{1,0:T(8,128)(2,1)} %heads.1) | copy-start | bytes 3145732
  2.7 0.8 %copy-start.1 = (bf16[32,1024]{1,0:T(8,128)(2,1)S(1)}, bf16[32,1024]{1,0:T(8,128)(2,1)}, u32[]{:S(2)}) copy-start(bf16[32,1024]{1,0:T(8,128)(2,1)} %resid.1) | copy-start | bytes 196612
  3.6 0.7 %copy-start.2 = (f32[1024]{0:T(1024)S(1)}, f32[1024]{0:T(1024)}, u32[]{:S(2)}) copy-start(f32[1024]{0:T(1024)} %param.12) | copy-start | bytes 12292

commit v2 on v1

--- a/solution.py
+++ b/solution.py
@@ -119,9 +119,9 @@
 
 
 def dense_kernel(
-    sizes, resid, heads, proj, gain, ids, scores, w_gate, w_up, w_down, out,
-    heads_v, proj_v, gate_v, up_v, down_v, rs_out, rs_in, mixed, rows, sq_out, sq_in, info,
-    core_out, core_in, own, y_out, y_in, active, pair_out, pair_in, part_out, part_in,
+    sizes, resid_hbm, heads, proj, gain_hbm, ids_hbm, scores_hbm, w_gate, w_up, w_down, out,
+    resid, gain, ids, scores, heads_v, proj_v, gate_v, up_v, down_v, rs_out, rs_in, mixed, rows, sq_out, sq_in, info,
+    core_out, core_in, own, y_out, y_in, active, kept_down, pair_out, pair_in, part_out, part_in,
     local_sem, send_sem, recv_sem,
 ):
     groups, tp_count, parts, out_parts = sizes
@@ -173,29 +173,41 @@
     get_heads = fetch(heads, heads_v)
     half = depth // 2
     get_proj = [
-        [
-            fetch(
-                proj.at[pl.ds(k * half, half), pl.ds(c * piece, piece)],
-                proj_v.at[c, pl.ds(k * half, half)],
-            )
-            for k in range(2)
-        ]
+        fetch(
+            proj.at[pl.ds(k * half, half), pl.ds(c * piece, piece)],
+            proj_v.at[c, pl.ds(k * half, half)],
+        )
         for c in range(parts)
+        for k in range(2)
+    ]
+    get_small = [
+        fetch(ids_hbm, ids), fetch(scores_hbm, scores), fetch(gain_hbm, gain),
+        fetch(resid_hbm, resid),
     ]
     get_gate = fetch(w_gate.at[0], gate_v)
     get_up = fetch(w_up.at[0], up_v)
     get_down = fetch(w_down.at[0], down_v)
-    get_heads.start()
-    for c in range(min(2, parts)):
-        for copy in get_proj[c]:
-            copy.start()
+    queue = get_proj + [get_gate, get_up, get_down]
+    for copy in [get_heads] + queue[:2] + get_small + queue[2:3]:
+        copy.start()
+    for copy in get_small:
+        copy.wait()
 
     lane = lax.broadcasted_iota(jnp.int32, (block, LANES), 1)
+    square_row = lax.broadcasted_iota(jnp.int32, (block, block), 0)
+    square_lane = lax.broadcasted_iota(jnp.int32, (block, block), 1)
+    expert_count = ids.shape[0]
+
+    def upright(row):
+        return jnp.sum(jnp.where(square_row == square_lane, row, 0.0), axis=1, keepdims=True)
+
     score = scores[...].astype(jnp.float32)
-    score = route_scale * score / jnp.sum(score, axis=1, keepdims=True)
+    score = route_scale * score / jnp.sum(score, axis=0, keepdims=True)
+    named = ids[...].astype(jnp.float32)
     weights = jnp.zeros((block, LANES), jnp.float32)
-    for k in range(ids.shape[1]):
-        weights += jnp.where(ids[:, k : k + 1] == lane, score[:, k : k + 1], 0.0)
+    for k in range(expert_count):
+        column = upright(named[k : k + 1]).astype(jnp.int32)
+        weights += jnp.where(column == lane, upright(score[k : k + 1]), 0.0)
 
     rs, spread, forward = {}, {}, {}
     keep = [None] * parts
@@ -221,18 +233,20 @@
             forward[c, d] = send(here, rows.at[1, d, :, columns], at_x)
 
     for c in range(parts):
-        if c == 0:
-            get_heads.wait()
-        for copy in get_proj[c]:
-            copy.wait()
-        if c + 2 < parts:
-            for copy in get_proj[c + 2]:
-                copy.start()
-        if c + 2 == parts or parts == 1:
-            get_gate.start()
-            get_up.start()
-            get_down.start()
-        share = jnp.dot(heads_v[...], proj_v[c], preferred_element_type=jnp.float32)
+        share = None
+        for k in range(2):
+            n = 2 * c + k
+            queue[n].wait()
+            if n + 3 < len(queue):
+                queue[n + 3].start()
+            if n == 0:
+                get_heads.wait()
+            term = jnp.dot(
+                heads_v[:, pl.ds(k * half, half)],
+                proj_v[c, pl.ds(k * half, half)],
+                preferred_element_type=jnp.float32,
+            )
+            share = term if share is None else share + term
         low, high = share[:block], share[block:]
         keep[c] = jnp.where(l == 0, low, high)
         rs_out[c] = jnp.where(l == 0, high, low).astype(jnp.bfloat16)
@@ -241,8 +255,6 @@
         rs[c] = send(rs_out.at[c], rs_in.at[c], at_x)
         if c >= 1:
             settle(c - 1)
-        if c >= 2:
-            pass_on(c - 2)
     settle(parts - 1)
 
     sq_out[...] = jnp.broadcast_to(square[0], sq_out.shape)
@@ -250,21 +262,22 @@
         send(sq_out, sq_in.at[r - 1], {"tp": lax.rem(t + r, tp_count)})
         for r in range(1, tp_count)
     ]
-    if parts >= 2:
-        pass_on(parts - 2)
-    pass_on(parts - 1)
-    total_square = sq_out[...]
-    for r, copy in enumerate(sums):
-        copy.wait_recv()
-        total_square += sq_in[r]
-    inverse = lax.rsqrt(total_square / (width * tp_count) + norm_eps)
-    expert_count = ids.shape[1]
-    info[0, 0] = jnp.where(lane < expert_count, weights, inverse)
+    for c in range(parts):
+        pass_on(c)
+
     told = {}
-    for d in range(groups):
-        told[1, d] = send(info.at[0, 0], info.at[1, d], {**at_group(d), **at_x})
-    for d in range(1, groups):
-        told[0, d] = send(info.at[0, 0], info.at[0, d], at_group(d))
+
+    def tell():
+        total_square = sq_out[...]
+        for r, copy in enumerate(sums):
+            copy.wait_recv()
+            total_square += sq_in[r]
+        inverse = lax.rsqrt(total_square / (width * tp_count) + norm_eps)
+        info[0, 0] = jnp.where(lane < expert_count, weights, inverse)
+        for d in range(groups):
+            told[1, d] = send(info.at[0, 0], info.at[1, d], {**at_group(d), **at_x})
+        for d in range(1, groups):
+            told[0, d] = send(info.at[0, 0], info.at[0, d], at_group(d))
 
     get_gate.wait()
     get_up.wait()
@@ -338,26 +351,27 @@
             total = part if total is None else total + part
         return total
 
+    give(0)
+    tell()
+    hold(0)
+    cross(0)
     give(1)
     hold(1)
-    give(0)
     cross(1)
-    hold(0)
-    cross(0)
     get_down.wait()
+    activate(0)
+    hand_over(0)
     activate(1)
-    activate(0)
+    for c in range(out_parts):
+        kept_down[c] = down(0, c)
     hand_over(1)
     across, home = {}, {}
     for c in range(out_parts):
         pair_out[c] = down(1, c).astype(jnp.bfloat16)
         across[c] = send(pair_out.at[c], pair_in.at[c], at_x)
-        if c == 0:
-            hand_over(0)
     for c in range(out_parts):
-        summed = down(0, c)
         across[c].wait_recv()
-        summed += pair_in[c].astype(jnp.float32)
+        summed = kept_down[c] + pair_in[c].astype(jnp.float32)
         part_out[c] = summed.astype(jnp.bfloat16).reshape(groups, block, out_piece)
         for d in range(1, groups):
             home[c, d] = send(part_out.at[c, d], part_in.at[c, d - 1], at_group(-d))
@@ -379,22 +393,25 @@
     ff = w_gate.shape[2]
     fpiece = ff // tp_count
     tall = groups * block
-    parts, out_parts = 4, 2
+    parts, out_parts = 4, 4
     piece, out_piece = width // parts, width // out_parts
     bf16, f32 = jnp.bfloat16, jnp.float32
-    local_copies = 4 + 2 * parts
+    local_copies = 8 + 2 * parts
     remote_copies = (
         parts + parts * (2 * groups - 1) + (tp_count - 1) + (2 * groups - 1) + 4 + 2 + 6
         + out_parts * groups
     )
     vmem = pl.BlockSpec(memory_space=pltpu.VMEM)
-    anywhere = pl.BlockSpec(memory_space=pl.ANY)
     return pl.pallas_call(
         functools.partial(dense_kernel, (groups, tp_count, parts, out_parts)),
         out_shape=jax.ShapeDtypeStruct(resid_in.shape, bf16),
-        in_specs=[vmem, anywhere, anywhere, vmem, vmem, vmem, anywhere, anywhere, anywhere],
+        in_specs=[pl.BlockSpec(memory_space=pltpu.HBM)] * 9,
         out_specs=vmem,
         scratch_shapes=[
+            pltpu.VMEM((block, width), bf16),
+            pltpu.VMEM((1, width), f32),
+            pltpu.VMEM(expert_ids.shape[::-1], jnp.int32),
+            pltpu.VMEM(gate_scores.shape[::-1], jnp.int32),
             pltpu.VMEM(heads_shape, bf16),
             pltpu.VMEM((parts, heads_shape[1], piece), bf16),
             pltpu.VMEM((width, ff), bf16),
@@ -413,6 +430,7 @@
             pltpu.VMEM((2, 2, tall, fpiece), bf16),
             pltpu.VMEM((2, 2, tall, fpiece), bf16),
             pltpu.VMEM((2, 4, tall, fpiece), bf16),
+            pltpu.VMEM((out_parts, tall, out_piece), f32),
             pltpu.VMEM((out_parts, tall, out_piece), bf16),
             pltpu.VMEM((out_parts, tall, out_piece), bf16),
             pltpu.VMEM((out_parts, groups, block, out_piece), bf16),
@@ -422,10 +440,10 @@
             pltpu.SemaphoreType.DMA((remote_copies,)),
         ],
         compiler_params=pltpu.CompilerParams(
-            collective_id=0, has_side_effects=True, vmem_limit_bytes=52 * 1024 * 1024
+            collective_id=0, has_side_effects=True, vmem_limit_bytes=64 * 1024 * 1024
         ),
     )(
-        resid_in, attn_heads, out_proj, norm_gain.reshape(1, width), expert_ids, gate_scores,
+        resid_in, attn_heads, out_proj, norm_gain.reshape(1, width), expert_ids.T, gate_scores.T,
         w_gate, w_up, w_down,
     )
 

time: 56.7 us -> 49.7 us (0.88)
  Pallas kernels: 51.5 us -> 48 us
  local copies, waits for them, and re-layouts: 4.9 us -> 1.47 us
    pallas_call x1, Pallas kernels: 51.5 us -> 48 us  [dense(): pl.pallas_call(functools.partial(dense_kernel, (groups, tp_count, parts,...]
    unnamed x9 -> x1, local copies, waits for them, and re-layouts: 4.9 us -> 1.47 us
where the time goes in v2:
time: 49.7 us; the launch traced here: 49.5 us
  Pallas kernels  48 us (97%)
  local copies, waits for them, and re-layouts  1.47 us (3%)
    pallas_call x1, Pallas kernels, dense(): pl.pallas_call(functools.partial(dense_kernel, (groups, tp_count, parts,...  48 us
    unnamed x1, local copies, waits for them, and re-layouts  1.47 us

profile of v2, /device:TPU:0, one launch (start us, length us, event | category | flops | bytes accessed | tf_op | source)
XLA Modules:
  0.0 49.5 jit_solution(16233369942380194355)
XLA Ops:
  0.0 48.0 %shard_map.91 = bf16[32,1024]{1,0:T(8,128)(2,1)} custom-call(bf16[32,1024]{1,0:T(8,128)(2,1)} %resid_hbm.1, bf16[64,8192]{1,0:T(8,128)(2,1)} %heads.1, bf16[8192,1024]{1,0:T(8,128)(2,1)} %proj.1, f32[1,1024]{1,0:T(1,128)} %bitcast.3, s32[8,32]{1,0:T(8,128)} %bitcast.4, s32[8,32]{1,0:T(8,128)} %bitcast.5, bf16[1,1024,1024]{2,1,0:T(8,128)(2,1)} %w_gate.1, ...), custom_call_target="tpu_custom_call" | custom-call | tf_op jit(solution)/shard_map/pallas_call | solution.py:405
  48.0 1.5 %copy.11 = bf16[32,1024]{1,0:T(8,128)(2,1)} copy(bf16[32,1024]{1,0:T(8,128)(2,1)} %shard_map.91) | data formatting | bytes 131072

commit v3 on v2

--- a/solution.py
+++ b/solution.py
@@ -255,6 +255,9 @@
         rs[c] = send(rs_out.at[c], rs_in.at[c], at_x)
         if c >= 1:
             settle(c - 1)
+    early = max(parts - 2, 0)
+    for c in range(early):
+        pass_on(c)
     settle(parts - 1)
 
     sq_out[...] = jnp.broadcast_to(square[0], sq_out.shape)
@@ -262,7 +265,7 @@
         send(sq_out, sq_in.at[r - 1], {"tp": lax.rem(t + r, tp_count)})
         for r in range(1, tp_count)
     ]
-    for c in range(parts):
+    for c in range(early, parts):
         pass_on(c)
 
     told = {}
@@ -335,17 +338,15 @@
         from_y[side].wait_recv()
         relay[side] = send(active.at[side, 2], active.at[side, 3], at_core)
 
-    def down(side, c):
+    places = (t, core_peer, y_peer, diagonal)
+
+    def down(side, c, first, last):
         columns = pl.ds(c * out_piece, out_piece)
         total = None
-        for n, q in enumerate((t, core_peer, y_peer, diagonal)):
-            if c == 0 and n == 1:
-                from_core[side].wait_recv()
-            if c == 0 and n == 3:
-                relay[side].wait_recv()
+        for n in range(first, last):
             part = jnp.dot(
                 active[side, n],
-                down_v[pl.ds(pl.multiple_of(q * fpiece, fpiece), fpiece), columns],
+                down_v[pl.ds(pl.multiple_of(places[n] * fpiece, fpiece), fpiece), columns],
                 preferred_element_type=jnp.float32,
             )
             total = part if total is None else total + part
@@ -360,18 +361,29 @@
     cross(1)
     get_down.wait()
     activate(0)
+    activate(1)
     hand_over(0)
-    activate(1)
-    for c in range(out_parts):
-        kept_down[c] = down(0, c)
+    from_core[0].wait_recv()
+    for c in range(out_parts):
+        kept_down[0, c] = down(0, c, 0, 3)
     hand_over(1)
+    from_core[1].wait_recv()
+    for c in range(out_parts):
+        kept_down[1, c] = down(1, c, 0, 3)
+    relay[1].wait_recv()
     across, home = {}, {}
-    for c in range(out_parts):
-        pair_out[c] = down(1, c).astype(jnp.bfloat16)
+    sent = len(started)
+    for c in range(out_parts):
+        pair_out[c] = (kept_down[1, c] + down(1, c, 3, 4)).astype(jnp.bfloat16)
         across[c] = send(pair_out.at[c], pair_in.at[c], at_x)
+    relay[0].wait_recv()
+    for c in range(out_parts):
+        kept_down[0, c] += down(0, c, 3, 4)
+    for copy in started[:sent]:
+        copy.wait_send()
     for c in range(out_parts):
         across[c].wait_recv()
-        summed = kept_down[c] + pair_in[c].astype(jnp.float32)
+        summed = kept_down[0, c] + pair_in[c].astype(jnp.float32)
         part_out[c] = summed.astype(jnp.bfloat16).reshape(groups, block, out_piece)
         for d in range(1, groups):
             home[c, d] = send(part_out.at[c, d], part_in.at[c, d - 1], at_group(-d))
@@ -382,7 +394,7 @@
             home[c, d].wait_recv()
             total += part_in[c, d - 1].astype(jnp.float32)
         out[:, columns] = total.astype(out.dtype)
-    for copy in started:
+    for copy in started[sent:]:
         copy.wait_send()
 
 
@@ -430,7 +442,7 @@
             pltpu.VMEM((2, 2, tall, fpiece), bf16),
             pltpu.VMEM((2, 2, tall, fpiece), bf16),
             pltpu.VMEM((2, 4, tall, fpiece), bf16),
-            pltpu.VMEM((out_parts, tall, out_piece), f32),
+            pltpu.VMEM((2, out_parts, tall, out_piece), f32),
             pltpu.VMEM((out_parts, tall, out_piece), bf16),
             pltpu.VMEM((out_parts, tall, out_piece), bf16),
             pltpu.VMEM((out_parts, groups, block, out_piece), bf16),

time: 49.7 us -> 49.1 us (0.988)
  Pallas kernels: 48 us -> 47.4 us
    pallas_call x1, Pallas kernels: 48 us -> 47.4 us  [dense(): pl.pallas_call(functools.partial(dense_kernel, (groups, tp_count, parts,...]
where the time goes in v3:
time: 49.1 us; the launch traced here: 48.9 us
  Pallas kernels  47.4 us (97%)
  local copies, waits for them, and re-layouts  1.47 us (3%)
    pallas_call x1, Pallas kernels, dense(): pl.pallas_call(functools.partial(dense_kernel, (groups, tp_count, parts,...  47.4 us
    unnamed x1, local copies, waits for them, and re-layouts  1.47 us

profile of v3, /device:TPU:0, one launch (start us, length us, event | category | flops | bytes accessed | tf_op | source)
XLA Modules:
  0.0 48.9 jit_solution(8592412824254168191)
XLA Ops:
  0.0 47.4 %shard_map.91 = bf16[32,1024]{1,0:T(8,128)(2,1)} custom-call(bf16[32,1024]{1,0:T(8,128)(2,1)} %resid_hbm.1, bf16[64,8192]{1,0:T(8,128)(2,1)} %heads.1, bf16[8192,1024]{1,0:T(8,128)(2,1)} %proj.1, f32[1,1024]{1,0:T(1,128)} %bitcast.3, s32[8,32]{1,0:T(8,128)} %bitcast.4, s32[8,32]{1,0:T(8,128)} %bitcast.5, bf16[1,1024,1024]{2,1,0:T(8,128)(2,1)} %w_gate.1, ...), custom_call_target="tpu_custom_call" | custom-call | tf_op jit(solution)/shard_map/pallas_call | solution.py:417
  47.4 1.5 %copy.11 = bf16[32,1024]{1,0:T(8,128)(2,1)} copy(bf16[32,1024]{1,0:T(8,128)(2,1)} %shard_map.91) | data formatting | bytes 131072

commit v4 on v3

--- a/solution.py
+++ b/solution.py
@@ -171,14 +171,15 @@
         return copy
 
     get_heads = fetch(heads, heads_v)
-    half = depth // 2
+    splits = 8 // parts
+    share_depth = depth // splits
     get_proj = [
         fetch(
-            proj.at[pl.ds(k * half, half), pl.ds(c * piece, piece)],
-            proj_v.at[c, pl.ds(k * half, half)],
+            proj.at[pl.ds(k * share_depth, share_depth), pl.ds(c * piece, piece)],
+            proj_v.at[c, pl.ds(k * share_depth, share_depth)],
         )
         for c in range(parts)
-        for k in range(2)
+        for k in range(splits)
     ]
     get_small = [
         fetch(ids_hbm, ids), fetch(scores_hbm, scores), fetch(gain_hbm, gain),
@@ -234,16 +235,16 @@
 
     for c in range(parts):
         share = None
-        for k in range(2):
-            n = 2 * c + k
+        for k in range(splits):
+            n = splits * c + k
             queue[n].wait()
             if n + 3 < len(queue):
                 queue[n + 3].start()
             if n == 0:
                 get_heads.wait()
             term = jnp.dot(
-                heads_v[:, pl.ds(k * half, half)],
-                proj_v[c, pl.ds(k * half, half)],
+                heads_v[:, pl.ds(k * share_depth, share_depth)],
+                proj_v[c, pl.ds(k * share_depth, share_depth)],
                 preferred_element_type=jnp.float32,
             )
             share = term if share is None else share + term
@@ -405,10 +406,10 @@
     ff = w_gate.shape[2]
     fpiece = ff // tp_count
     tall = groups * block
-    parts, out_parts = 4, 4
+    parts, out_parts = 2, 2
     piece, out_piece = width // parts, width // out_parts
     bf16, f32 = jnp.bfloat16, jnp.float32
-    local_copies = 8 + 2 * parts
+    local_copies = 16
     remote_copies = (
         parts + parts * (2 * groups - 1) + (tp_count - 1) + (2 * groups - 1) + 4 + 2 + 6
         + out_parts * groups

time: 49.1 us -> 49.4 us (level)
  no operation moved by 1% of the time
where the time goes in v4:
time: 49.4 us; the launch traced here: 49.2 us
  Pallas kernels  47.8 us (97%)
  local copies, waits for them, and re-layouts  1.47 us (3%)
    pallas_call x1, Pallas kernels, dense(): pl.pallas_call(functools.partial(dense_kernel, (groups, tp_count, parts,...  47.8 us
    unnamed x1, local copies, waits for them, and re-layouts  1.47 us

profile of v4, /device:TPU:0, one launch (start us, length us, event | category | flops | bytes accessed | tf_op | source)
XLA Modules:
  0.0 49.2 jit_solution(15254960103587796411)
XLA Ops:
  0.0 47.8 %shard_map.91 = bf16[32,1024]{1,0:T(8,128)(2,1)} custom-call(bf16[32,1024]{1,0:T(8,128)(2,1)} %resid_hbm.1, bf16[64,8192]{1,0:T(8,128)(2,1)} %heads.1, bf16[8192,1024]{1,0:T(8,128)(2,1)} %proj.1, f32[1,1024]{1,0:T(1,128)} %bitcast.3, s32[8,32]{1,0:T(8,128)} %bitcast.4, s32[8,32]{1,0:T(8,128)} %bitcast.5, bf16[1,1024,1024]{2,1,0:T(8,128)(2,1)} %w_gate.1, ...), custom_call_target="tpu_custom_call" | custom-call | tf_op jit(solution)/shard_map/pallas_call | solution.py:418
  47.8 1.5 %copy.11 = bf16[32,1024]{1,0:T(8,128)(2,1)} copy(bf16[32,1024]{1,0:T(8,128)(2,1)} %shard_map.91) | data formatting | bytes 131072

commit v5 on v4

--- a/solution.py
+++ b/solution.py
@@ -334,10 +334,10 @@
         active[side, 0] = value.astype(jnp.bfloat16)
         from_y[side] = send(active.at[side, 0], active.at[side, 2], at_y)
         from_core[side] = send(active.at[side, 0], active.at[side, 1], at_core)
+        relay[side] = send(active.at[side, 0], active.at[side, 3], {"tp": diagonal})
 
     def hand_over(side):
         from_y[side].wait_recv()
-        relay[side] = send(active.at[side, 2], active.at[side, 3], at_core)
 
     places = (t, core_peer, y_peer, diagonal)
 

time: 49.4 us -> 49.8 us (level)
  no operation moved by 1% of the time
where the time goes in v5:
time: 49.8 us; the launch traced here: 49.7 us
  Pallas kernels  48.2 us (97%)
  local copies, waits for them, and re-layouts  1.47 us (3%)
    pallas_call x1, Pallas kernels, dense(): pl.pallas_call(functools.partial(dense_kernel, (groups, tp_count, parts,...  48.2 us
    unnamed x1, local copies, waits for them, and re-layouts  1.47 us

profile of v5, /device:TPU:0, one launch (start us, length us, event | category | flops | bytes accessed | tf_op | source)
XLA Modules:
  0.0 49.7 jit_solution(2726269639702275932)
XLA Ops:
  0.0 48.2 %shard_map.91 = bf16[32,1024]{1,0:T(8,128)(2,1)} custom-call(bf16[32,1024]{1,0:T(8,128)(2,1)} %resid_hbm.1, bf16[64,8192]{1,0:T(8,128)(2,1)} %heads.1, bf16[8192,1024]{1,0:T(8,128)(2,1)} %proj.1, f32[1,1024]{1,0:T(1,128)} %bitcast.3, s32[8,32]{1,0:T(8,128)} %bitcast.4, s32[8,32]{1,0:T(8,128)} %bitcast.5, bf16[1,1024,1024]{2,1,0:T(8,128)(2,1)} %w_gate.1, ...), custom_call_target="tpu_custom_call" | custom-call | tf_op jit(solution)/shard_map/pallas_call | solution.py:418
  48.2 1.5 %copy.11 = bf16[32,1024]{1,0:T(8,128)(2,1)} copy(bf16[32,1024]{1,0:T(8,128)(2,1)} %shard_map.91) | data formatting | bytes 131072
